TPU v7x, 128 devices: a whole 4x4x4 slice. The times are simulated.
128 devices in a mesh: ta: 2 (over core), ha: 8 (over x_lo, z), wa: 8 (over y, x_hi).
Axes of the slice: x: 4 (x_hi: 2, x_lo: 2; x = x_hi * 2 + x_lo), y: 4, z: 4, core: 2. Of those that a mesh axis runs over, the one named last changes fastest.
Arguments:
- queries: bfloat16 [48, 64, 64, 256], P(('ta', 'ha'), None, 'wa'), may hold values from -100 to 100
- key_field: bfloat16 [48, 64, 64, 256], P(('ta', 'ha'), None, 'wa'), may hold values from -4.1 to 4.1
- value_field: bfloat16 [48, 64, 64, 256], P(('ta', 'ha'), None, 'wa'), may hold values from -6 to 6
Outputs:
- attended: bfloat16 [48, 64, 64, 256], P(('ta', 'ha'), None, 'wa')
All inputs are finite; a program needn't handle non-finite values.
Results may differ from a plain program's by a relative error of at most 0.0048.
Values may be sent and summed in bfloat16 or wider, within the bound.
A program may use at most 128 MiB of HBM per device.

v0:
```python
import jax
import jax.numpy as jnp
from jax import lax
from jax.sharding import PartitionSpec as P

HEAD = 128
HEADS = 2
TT = 6
TH = 8
TW = 8


def padded(shard, sides, width):
    for axis, dim in sides:
        size, length = (lax.axis_size(axis), shard.shape[dim])
        up = [(i, (i + 1) % size) for i in range(size - 1)]
        down = [(j, i) for i, j in up]
        last = lax.slice_in_dim(shard, length - width, length, axis=dim)
        initial = lax.slice_in_dim(shard, 0, width, axis=dim)
        before = lax.ppermute(last, axis, up)
        after = lax.ppermute(initial, axis, down)
        shard = jnp.concatenate([before, shard, after], axis=dim)
    return shard


def shortened(shard):

    def short(part):
        return part.astype(jnp.bfloat16) if part.dtype == jnp.float32 else part

    return jax.tree.map(short, shard)


def head_attention(query_part, key_part, value_part, allowed):
    scores = jnp.einsum(
        "qd,kd->qk", query_part, key_part, preferred_element_type=jnp.float32
    ) * query_part.shape[1] ** (-0.5)
    scores = jnp.where(allowed[None, :], scores, -jnp.inf)
    largest = jnp.max(scores, axis=1, keepdims=True)
    expon = jnp.exp(scores - largest)
    totals = jnp.sum(expon, axis=1, keepdims=True)
    weights = expon.astype(jnp.bfloat16)
    summed = jnp.dot(weights, value_part, preferred_element_type=jnp.float32)
    return (summed / totals).astype(jnp.bfloat16)


def tile_view(block):
    leading = block.shape[:-4]
    frames = block.shape[-4]
    return block.reshape(leading + (frames // TT, 1, 1, TT * TH * TW, block.shape[-1]))


def neighbour_tiles(pair_tiles):
    return padded(pair_tiles, (("ta", 1), ("ha", 2), ("wa", 3)), 1)


def per_device(queries, key_field, value_field):
    arrived = lax.all_to_all(
        jnp.stack([queries, key_field, value_field]), "ha", split_axis=2, concat_axis=1, tiled=True
    )
    query_cube = arrived[0]
    extended = neighbour_tiles(tile_view(arrived[1:]))
    query_tiles = tile_view(query_cube)[:, 0, 0]
    tiles_t = query_tiles.shape[0]
    tile_len = query_tiles.shape[1]
    channels = query_tiles.shape[2]
    frame_pos = lax.axis_index("ta") * tiles_t + jnp.arange(tiles_t + 2, dtype=jnp.int32) - 1
    valid_t = (frame_pos >= 0) & (frame_pos < tiles_t * lax.axis_size("ta"))
    height_pos = lax.axis_index("ha") + jnp.arange(3, dtype=jnp.int32) - 1
    valid_h = (height_pos >= 0) & (height_pos < lax.axis_size("ha"))
    width_pos = lax.axis_index("wa") + jnp.arange(3, dtype=jnp.int32) - 1
    valid_w = (width_pos >= 0) & (width_pos < lax.axis_size("wa"))

    def attend_tile(tile_idx):
        window = lax.dynamic_slice_in_dim(extended, tile_idx, 3, 1).reshape(
            2, 27 * tile_len, channels
        )
        allowed = (
            lax.dynamic_slice_in_dim(valid_t, tile_idx, 3)[:, None, None]
            & valid_h[None, :, None]
            & valid_w[None, None, :]
        )
        allowed = jnp.broadcast_to(allowed.reshape(27, 1), (27, tile_len)).reshape(27 * tile_len)
        query_rows = lax.dynamic_index_in_dim(query_tiles, tile_idx, 0, keepdims=False)
        outputs = []
        for head_num in range(HEADS):
            offset = head_num * HEAD
            outputs.append(
                head_attention(
                    query_rows[:, offset : offset + HEAD],
                    window[0, :, offset : offset + HEAD],
                    window[1, :, offset : offset + HEAD],
                    allowed,
                )
            )
        return jnp.concatenate(outputs, axis=1)

    blocks = lax.map(attend_tile, jnp.arange(tiles_t, dtype=jnp.int32))
    out_cube = blocks.reshape(query_cube.shape)
    return lax.all_to_all(
        shortened(out_cube), "ha", split_axis=0, concat_axis=1, tiled=True
    ).astype(out_cube.dtype)


def solution(mesh):
    in_specs = (
        P(("ta", "ha"), None, "wa", None),
        P(("ta", "ha"), None, "wa", None),
        P(("ta", "ha"), None, "wa", None),
    )
    out_specs = P(("ta", "ha"), None, "wa", None)
    return jax.shard_map(
        per_device, mesh=mesh, in_specs=in_specs, out_specs=out_specs, check_vma=False
    )
```

profile of v0, /device:TPU:1, one launch (start us, length us, event | category | flops | bytes accessed | tf_op | source)
XLA Modules:
  0.0 716.1 jit_solution(1300733896888958193)
XLA Ops:
  0.0 1.2 copy.22
  1.2 1.5 copy_bitcast_fusion
  2.7 0.2 pad_maximum_fusion.2
  2.9 35.1 %all_to_all.33 = bf16[3,3,64,8,256]{4,3,1,0,2:T(8,128)(2,1)S(1)} all-to-all(bf16[3,3,64,8,256]{4,3,1,0,2:T(8,128)(2,1)S(1)} %pad_maximum_fusion.2), channel_id=1, replica_groups=mesh['ta'=2,'ha'=8,'wa'=8] {'ha'}, dimensions={2} | all-to-all | bytes 4718592 | tf_op jit(solution)/shard_map/all_to_all | solution.py:58
  38.0 1.5 copy-done
  39.6 0.2 copy.14
  39.9 1.3 collective-permute-start
  41.2 4.4 collective-permute-start.1
  45.6 1.3 collective-permute-done.1
  46.9 0.3 pad_maximum_fusion.3
  47.2 2.0 collective-permute-start.2
  49.2 1.3 collective-permute-start.3
  50.5 48.8 %collective-permute-done.2 = bf16[2,6,1,1,384,256]{5,4,3,2,1,0:T(8,128)(2,1)S(1)} collective-permute-done((bf16[2,6,1,1,384,256]{5,4,3,2,1,0:T(8,128)(2,1)S(1)}, bf16[2,6,1,1,384,256]{5,4,3,2,1,0:T(8,128)(2,1)S(1)}, u32[]{:S(2)}, u32[]{:S(2)}) %collective-permute-start.2) | collective-permute-done | bytes 2359328 | tf_op jit(solution)/shard_map/ppermute | solution.py:20
  99.3 3.9 collective-permute-done.3
  103.2 3.7 pad_maximum_fusion.1
  106.9 7.2 %collective-permute-start.4 = (bf16[2,6,3,1,384,256]{5,4,3,2,1,0:T(8,128)(2,1)}, bf16[2,6,3,1,384,256]{5,4,3,2,1,0:T(8,128)(2,1)}, u32[]{:S(2)}, u32[]{:S(2)}) collective-permute-start(bf16[2,6,3,1,384,256]{5,4,3,2,1,0:T(8,128)(2,1)} %pad_maximum_fusion.1), channel_id=1, source_target_pairs={{0,1},{1,2},{2,3},{3,4},{4,5},{5,6},{6,7},{8,9},{9,10},{10,11},{11... | collective-permute-start | bytes 21233672 | tf_op jit(solution)/shard_map/ppermute | solution.py:20
  114.1 1.3 collective-permute-start.5
  115.4 1.2 slice.48
  116.7 145.0 %collective-permute-done.4 = bf16[2,6,3,1,384,256]{5,4,3,2,1,0:T(8,128)(2,1)} collective-permute-done((bf16[2,6,3,1,384,256]{5,4,3,2,1,0:T(8,128)(2,1)}, bf16[2,6,3,1,384,256]{5,4,3,2,1,0:T(8,128)(2,1)}, u32[]{:S(2)}, u32[]{:S(2)}) %collective-permute-start.4) | collective-permute-done | bytes 7077920 | tf_op jit(solution)/shard_map/ppermute | solution.py:20
  261.7 153.9 %collective-permute-done.5 = bf16[2,6,3,1,384,256]{5,4,3,2,1,0:T(8,128)(2,1)} collective-permute-done((bf16[2,6,3,1,384,256]{5,4,3,2,1,0:T(8,128)(2,1)}, bf16[2,6,3,1,384,256]{5,4,3,2,1,0:T(8,128)(2,1)}, u32[]{:S(2)}, u32[]{:S(2)}) %collective-permute-start.5) | collective-permute-done | bytes 7077920 | tf_op jit(solution)/shard_map/ppermute | solution.py:21
  415.7 14.5 %pad_maximum_fusion = bf16[2,6,3,3,384,256]{5,4,3,2,1,0:T(8,128)(2,1)} fusion(bf16[2,6,3,1,384,256]{5,4,3,2,1,0:T(8,128)(2,1)} %collective-permute-done.5, bf16[2,6,1,1,384,256]{5,4,3,2,1,0:T(8,128)(2,1)} %copy-done.2, bf16[2,1,1,1,384,256]{5,4,3,2,1,0:T(8,128)(2,1)S(1)} %collective-permute-done.1, bf16[2,4,1,1,384,256]{5,4,3,2,1,0:T(8,128)(2,1)S(1)} %bitcast.70, ...), kind=kLoop, calls=%fused_computation.34 | loop fusion | flops 63700992 | bytes 42467328 | tf_op jit(solution)/shard_map/concatenate | solution.py:22
  430.1 269.5 %while.11 = (s32[]{:T(128)}, bf16[4,384,256]{2,1,0:T(8,128)(2,1)}, s32[4]{0:T(128)S(1)}, pred[6]{0:T(512)(128)(4,1)S(1)}, bf16[4,384,256]{2,1,0:T(8,128)(2,1)S(1...) while((s32[]{:T(128)}, bf16[4,384,256]{2,1,0:T(8,128)(2,1)}, ...), condition=%wide.region_5.6_spmd.clone, body=%wide.region_0.5_spmd.clone.sunk | while | flops 4133190144 | bytes 129437928 | solution.py:98
  430.3 0.7 dynamic_slice.26
  433.3 9.4 %constant_dynamic-slice_fusion.2 = bf16[2,3,3,3,384,256]{5,4,3,2,1,0:T(8,128)(2,1)} fusion(bf16[2,6,3,3,384,256]{5,4,3,2,1,0:T(8,128)(2,1)} %get-tuple-element.185, s32[]{:T(128)S(6)} %select_n.23), kind=kLoop, calls=%fused_computation.33.clone.1 | loop fusion | bytes 21233668 | tf_op jit(solution)/shard_map/while/body/eval_jaxpr/dynamic_slice | solution.py:75
  444.0 9.5 %fusion.46 = (f32[384]{0:T(512)S(1)}, f32[384,10368]{1,0:T(8,128)}) fusion(bf16[2,10368,256]{2,1,0:T(8,128)(2,1)} %bitcast.63, bf16[384,256]{1,0:T(8,128)(2,1)S(1)} %dynamic-slice_bitcast_fusion.2, pred[10368]{0:T(1024)(128)(4,1)S(1)} %broadcast_in_dim.50), kind=kOutput, calls=%fused_computation.43.clone.1 | convolution fusion | flops 1031159424 | bytes 18690560 | tf_op jit(solution)/shard_map/while/body/eval_jaxpr/qd,kd->qk/dot_general | solution.py:35
  453.6 7.8 %fusion.47 = f32[384]{0:T(512)S(1)} fusion(f32[384,10368]{1,0:T(8,128)} %get-tuple-element.154, f32[384]{0:T(512)S(1)} %get-tuple-element.155), kind=kLoop, calls=%fused_computation.8.clone.1 | loop fusion | flops 7962240 | bytes 15928320 | tf_op jit(solution)/shard_map/while/body/eval_jaxpr/reduce_sum | solution.py:41
  461.3 9.1 %fusion.48 = bf16[384,128]{0,1:T(8,128)(2,1)S(1)} fusion(bf16[2,10368,256]{2,1,0:T(8,128)(2,1)} %bitcast.64, f32[384,10368]{1,0:T(8,128)} %get-tuple-element.154, f32[384]{0:T(512)S(1)} %get-tuple-element.155, f32[384]{0:T(512)S(1)} %fusion.47), kind=kOutput, calls=%fused_computation.21.clone.1 | convolution fusion | flops 1027276800 | bytes 18680832 | tf_op jit(solution)/shard_map/while/body/eval_jaxpr/dot_general | solution.py:43
  470.4 9.5 %fusion.43 = (f32[384]{0:T(512)S(1)}, f32[384,10368]{1,0:T(8,128)}) fusion(bf16[2,10368,256]{2,1,0:T(8,128)(2,1)} %bitcast.65, bf16[384,256]{1,0:T(8,128)(2,1)S(1)} %dynamic-slice_bitcast_fusion.2, pred[10368]{0:T(1024)(128)(4,1)S(1)} %broadcast_in_dim.50), kind=kOutput, calls=%fused_computation.42.clone.1 | convolution fusion | flops 1031159424 | bytes 18690560 | tf_op jit(solution)/shard_map/while/body/eval_jaxpr/qd,kd->qk/dot_general | solution.py:35
  479.9 7.8 %fusion.44 = f32[384]{0:T(512)S(1)} fusion(f32[384,10368]{1,0:T(8,128)} %get-tuple-element.152, f32[384]{0:T(512)S(1)} %get-tuple-element.153), kind=kLoop, calls=%fused_computation.10.clone.1 | loop fusion | flops 7962240 | bytes 15928320 | tf_op jit(solution)/shard_map/while/body/eval_jaxpr/reduce_sum | solution.py:41
  487.7 9.1 %fusion.45 = bf16[384,128]{0,1:T(8,128)(2,1)S(1)} fusion(bf16[2,10368,256]{2,1,0:T(8,128)(2,1)} %bitcast.66, f32[384,10368]{1,0:T(8,128)} %get-tuple-element.152, f32[384]{0:T(512)S(1)} %get-tuple-element.153, f32[384]{0:T(512)S(1)} %fusion.44), kind=kOutput, calls=%fused_computation.23.clone.1 | convolution fusion | flops 1027276800 | bytes 18680832 | tf_op jit(solution)/shard_map/while/body/eval_jaxpr/dot_general | solution.py:43
  496.8 0.1 copy.24
  497.0 0.7 constant_dynamic-update-slice_fusion.2
  497.7 0.7 dynamic_slice.26
  500.7 9.4 %constant_dynamic-slice_fusion.2 = bf16[2,3,3,3,384,256]{5,4,3,2,1,0:T(8,128)(2,1)} fusion(bf16[2,6,3,3,384,256]{5,4,3,2,1,0:T(8,128)(2,1)} %get-tuple-element.185, s32[]{:T(128)S(6)} %select_n.23), kind=kLoop, calls=%fused_computation.33.clone.1 | loop fusion | bytes 21233668 | tf_op jit(solution)/shard_map/while/body/eval_jaxpr/dynamic_slice | solution.py:75
  511.4 9.5 %fusion.46 = (f32[384]{0:T(512)S(1)}, f32[384,10368]{1,0:T(8,128)}) fusion(bf16[2,10368,256]{2,1,0:T(8,128)(2,1)} %bitcast.63, bf16[384,256]{1,0:T(8,128)(2,1)S(1)} %dynamic-slice_bitcast_fusion.2, pred[10368]{0:T(1024)(128)(4,1)S(1)} %broadcast_in_dim.50), kind=kOutput, calls=%fused_computation.43.clone.1 | convolution fusion | flops 1031159424 | bytes 18690560 | tf_op jit(solution)/shard_map/while/body/eval_jaxpr/qd,kd->qk/dot_general | solution.py:35
  520.9 7.8 %fusion.47 = f32[384]{0:T(512)S(1)} fusion(f32[384,10368]{1,0:T(8,128)} %get-tuple-element.154, f32[384]{0:T(512)S(1)} %get-tuple-element.155), kind=kLoop, calls=%fused_computation.8.clone.1 | loop fusion | flops 7962240 | bytes 15928320 | tf_op jit(solution)/shard_map/while/body/eval_jaxpr/reduce_sum | solution.py:41
  528.7 9.1 %fusion.48 = bf16[384,128]{0,1:T(8,128)(2,1)S(1)} fusion(bf16[2,10368,256]{2,1,0:T(8,128)(2,1)} %bitcast.64, f32[384,10368]{1,0:T(8,128)} %get-tuple-element.154, f32[384]{0:T(512)S(1)} %get-tuple-element.155, f32[384]{0:T(512)S(1)} %fusion.47), kind=kOutput, calls=%fused_computation.21.clone.1 | convolution fusion | flops 1027276800 | bytes 18680832 | tf_op jit(solution)/shard_map/while/body/eval_jaxpr/dot_general | solution.py:43
  537.8 9.5 %fusion.43 = (f32[384]{0:T(512)S(1)}, f32[384,10368]{1,0:T(8,128)}) fusion(bf16[2,10368,256]{2,1,0:T(8,128)(2,1)} %bitcast.65, bf16[384,256]{1,0:T(8,128)(2,1)S(1)} %dynamic-slice_bitcast_fusion.2, pred[10368]{0:T(1024)(128)(4,1)S(1)} %broadcast_in_dim.50), kind=kOutput, calls=%fused_computation.42.clone.1 | convolution fusion | flops 1031159424 | bytes 18690560 | tf_op jit(solution)/shard_map/while/body/eval_jaxpr/qd,kd->qk/dot_general | solution.py:35
  547.3 7.8 %fusion.44 = f32[384]{0:T(512)S(1)} fusion(f32[384,10368]{1,0:T(8,128)} %get-tuple-element.152, f32[384]{0:T(512)S(1)} %get-tuple-element.153), kind=kLoop, calls=%fused_computation.10.clone.1 | loop fusion | flops 7962240 | bytes 15928320 | tf_op jit(solution)/shard_map/while/body/eval_jaxpr/reduce_sum | solution.py:41
  555.0 9.1 %fusion.45 = bf16[384,128]{0,1:T(8,128)(2,1)S(1)} fusion(bf16[2,10368,256]{2,1,0:T(8,128)(2,1)} %bitcast.66, f32[384,10368]{1,0:T(8,128)} %get-tuple-element.152, f32[384]{0:T(512)S(1)} %get-tuple-element.153, f32[384]{0:T(512)S(1)} %fusion.44), kind=kOutput, calls=%fused_computation.23.clone.1 | convolution fusion | flops 1027276800 | bytes 18680832 | tf_op jit(solution)/shard_map/while/body/eval_jaxpr/dot_general | solution.py:43
  564.2 0.1 copy.24
  564.3 0.7 constant_dynamic-update-slice_fusion.2
  565.0 0.7 dynamic_slice.26
  568.0 9.4 %constant_dynamic-slice_fusion.2 = bf16[2,3,3,3,384,256]{5,4,3,2,1,0:T(8,128)(2,1)} fusion(bf16[2,6,3,3,384,256]{5,4,3,2,1,0:T(8,128)(2,1)} %get-tuple-element.185, s32[]{:T(128)S(6)} %select_n.23), kind=kLoop, calls=%fused_computation.33.clone.1 | loop fusion | bytes 21233668 | tf_op jit(solution)/shard_map/while/body/eval_jaxpr/dynamic_slice | solution.py:75
  578.7 9.5 %fusion.46 = (f32[384]{0:T(512)S(1)}, f32[384,10368]{1,0:T(8,128)}) fusion(bf16[2,10368,256]{2,1,0:T(8,128)(2,1)} %bitcast.63, bf16[384,256]{1,0:T(8,128)(2,1)S(1)} %dynamic-slice_bitcast_fusion.2, pred[10368]{0:T(1024)(128)(4,1)S(1)} %broadcast_in_dim.50), kind=kOutput, calls=%fused_computation.43.clone.1 | convolution fusion | flops 1031159424 | bytes 18690560 | tf_op jit(solution)/shard_map/while/body/eval_jaxpr/qd,kd->qk/dot_general | solution.py:35
  588.2 7.8 %fusion.47 = f32[384]{0:T(512)S(1)} fusion(f32[384,10368]{1,0:T(8,128)} %get-tuple-element.154, f32[384]{0:T(512)S(1)} %get-tuple-element.155), kind=kLoop, calls=%fused_computation.8.clone.1 | loop fusion | flops 7962240 | bytes 15928320 | tf_op jit(solution)/shard_map/while/body/eval_jaxpr/reduce_sum | solution.py:41
  596.0 9.1 %fusion.48 = bf16[384,128]{0,1:T(8,128)(2,1)S(1)} fusion(bf16[2,10368,256]{2,1,0:T(8,128)(2,1)} %bitcast.64, f32[384,10368]{1,0:T(8,128)} %get-tuple-element.154, f32[384]{0:T(512)S(1)} %get-tuple-element.155, f32[384]{0:T(512)S(1)} %fusion.47), kind=kOutput, calls=%fused_computation.21.clone.1 | convolution fusion | flops 1027276800 | bytes 18680832 | tf_op jit(solution)/shard_map/while/body/eval_jaxpr/dot_general | solution.py:43
  605.1 9.5 %fusion.43 = (f32[384]{0:T(512)S(1)}, f32[384,10368]{1,0:T(8,128)}) fusion(bf16[2,10368,256]{2,1,0:T(8,128)(2,1)} %bitcast.65, bf16[384,256]{1,0:T(8,128)(2,1)S(1)} %dynamic-slice_bitcast_fusion.2, pred[10368]{0:T(1024)(128)(4,1)S(1)} %broadcast_in_dim.50), kind=kOutput, calls=%fused_computation.42.clone.1 | convolution fusion | flops 1031159424 | bytes 18690560 | tf_op jit(solution)/shard_map/while/body/eval_jaxpr/qd,kd->qk/dot_general | solution.py:35
  614.6 7.8 %fusion.44 = f32[384]{0:T(512)S(1)} fusion(f32[384,10368]{1,0:T(8,128)} %get-tuple-element.152, f32[384]{0:T(512)S(1)} %get-tuple-element.153), kind=kLoop, calls=%fused_computation.10.clone.1 | loop fusion | flops 7962240 | bytes 15928320 | tf_op jit(solution)/shard_map/while/body/eval_jaxpr/reduce_sum | solution.py:41
  622.4 9.1 %fusion.45 = bf16[384,128]{0,1:T(8,128)(2,1)S(1)} fusion(bf16[2,10368,256]{2,1,0:T(8,128)(2,1)} %bitcast.66, f32[384,10368]{1,0:T(8,128)} %get-tuple-element.152, f32[384]{0:T(512)S(1)} %get-tuple-element.153, f32[384]{0:T(512)S(1)} %fusion.44), kind=kOutput, calls=%fused_computation.23.clone.1 | convolution fusion | flops 1027276800 | bytes 18680832 | tf_op jit(solution)/shard_map/while/body/eval_jaxpr/dot_general | solution.py:43
  631.5 0.1 copy.24
  631.6 0.7 constant_dynamic-update-slice_fusion.2
  632.3 0.7 dynamic_slice.26
  635.3 9.4 %constant_dynamic-slice_fusion.2 = bf16[2,3,3,3,384,256]{5,4,3,2,1,0:T(8,128)(2,1)} fusion(bf16[2,6,3,3,384,256]{5,4,3,2,1,0:T(8,128)(2,1)} %get-tuple-element.185, s32[]{:T(128)S(6)} %select_n.23), kind=kLoop, calls=%fused_computation.33.clone.1 | loop fusion | bytes 21233668 | tf_op jit(solution)/shard_map/while/body/eval_jaxpr/dynamic_slice | solution.py:75
  646.1 9.5 %fusion.46 = (f32[384]{0:T(512)S(1)}, f32[384,10368]{1,0:T(8,128)}) fusion(bf16[2,10368,256]{2,1,0:T(8,128)(2,1)} %bitcast.63, bf16[384,256]{1,0:T(8,128)(2,1)S(1)} %dynamic-slice_bitcast_fusion.2, pred[10368]{0:T(1024)(128)(4,1)S(1)} %broadcast_in_dim.50), kind=kOutput, calls=%fused_computation.43.clone.1 | convolution fusion | flops 1031159424 | bytes 18690560 | tf_op jit(solution)/shard_map/while/body/eval_jaxpr/qd,kd->qk/dot_general | solution.py:35
  655.6 7.8 %fusion.47 = f32[384]{0:T(512)S(1)} fusion(f32[384,10368]{1,0:T(8,128)} %get-tuple-element.154, f32[384]{0:T(512)S(1)} %get-tuple-element.155), kind=kLoop, calls=%fused_computation.8.clone.1 | loop fusion | flops 7962240 | bytes 15928320 | tf_op jit(solution)/shard_map/while/body/eval_jaxpr/reduce_sum | solution.py:41
  663.3 9.1 %fusion.48 = bf16[384,128]{0,1:T(8,128)(2,1)S(1)} fusion(bf16[2,10368,256]{2,1,0:T(8,128)(2,1)} %bitcast.64, f32[384,10368]{1,0:T(8,128)} %get-tuple-element.154, f32[384]{0:T(512)S(1)} %get-tuple-element.155, f32[384]{0:T(512)S(1)} %fusion.47), kind=kOutput, calls=%fused_computation.21.clone.1 | convolution fusion | flops 1027276800 | bytes 18680832 | tf_op jit(solution)/shard_map/while/body/eval_jaxpr/dot_general | solution.py:43
  672.4 9.5 %fusion.43 = (f32[384]{0:T(512)S(1)}, f32[384,10368]{1,0:T(8,128)}) fusion(bf16[2,10368,256]{2,1,0:T(8,128)(2,1)} %bitcast.65, bf16[384,256]{1,0:T(8,128)(2,1)S(1)} %dynamic-slice_bitcast_fusion.2, pred[10368]{0:T(1024)(128)(4,1)S(1)} %broadcast_in_dim.50), kind=kOutput, calls=%fused_computation.42.clone.1 | convolution fusion | flops 1031159424 | bytes 18690560 | tf_op jit(solution)/shard_map/while/body/eval_jaxpr/qd,kd->qk/dot_general | solution.py:35
  681.9 7.8 %fusion.44 = f32[384]{0:T(512)S(1)} fusion(f32[384,10368]{1,0:T(8,128)} %get-tuple-element.152, f32[384]{0:T(512)S(1)} %get-tuple-element.153), kind=kLoop, calls=%fused_computation.10.clone.1 | loop fusion | flops 7962240 | bytes 15928320 | tf_op jit(solution)/shard_map/while/body/eval_jaxpr/reduce_sum | solution.py:41
  689.7 9.1 %fusion.45 = bf16[384,128]{0,1:T(8,128)(2,1)S(1)} fusion(bf16[2,10368,256]{2,1,0:T(8,128)(2,1)} %bitcast.66, f32[384,10368]{1,0:T(8,128)} %get-tuple-element.152, f32[384]{0:T(512)S(1)} %get-tuple-element.153, f32[384]{0:T(512)S(1)} %fusion.44), kind=kOutput, calls=%fused_computation.23.clone.1 | convolution fusion | flops 1027276800 | bytes 18680832 | tf_op jit(solution)/shard_map/while/body/eval_jaxpr/dot_general | solution.py:43
  698.8 0.1 copy.24
  699.0 0.7 constant_dynamic-update-slice_fusion.2
  699.7 15.5 %all_to_all.34 = bf16[24,8,8,256]{3,2,1,0:T(8,128)(2,1)S(1)} all-to-all(bf16[24,8,8,256]{3,2,1,0:T(8,128)(2,1)} %bitcast.76), channel_id=1, replica_groups=mesh['ta'=2,'ha'=8,'wa'=8] {'ha'}, dimensions={0} | all-to-all | bytes 1572864 | tf_op jit(solution)/shard_map/all_to_all | solution.py:100
  715.1 1.0 copy.16
  (48 shorter events, 2.2 us)
Async XLA Ops:
  38.0 1.5 copy-start
  39.9 5.7 collective-permute-start
  41.2 5.7 collective-permute-start.1
  47.2 52.1 %collective-permute-start.2 = (bf16[2,6,1,1,384,256]{5,4,3,2,1,0:T(8,128)(2,1)S(1)}, bf16[2,6,1,1,384,256]{5,4,3,2,1,0:T(8,128)(2,1)S(1)}, u32[]{:S(2)}, u32[]{:S(2)}) collective-permute-start(bf16[2,6,1,1,384,256]{5,4,3,2,1,0:T(8,128)(2,1)S(1)} %pad_maximum_fusion.3), channel_id=1, source_target_pairs={{0,8},{8,16},{16,24},{24,32},{32,40},{40,48},{48,56},{1,9},{9,17},... | collective-permute-start | bytes 7077896 | tf_op jit(solution)/shard_map/ppermute | solution.py:20
  49.2 54.0 %collective-permute-start.3 = (bf16[2,6,1,1,384,256]{5,4,3,2,1,0:T(8,128)(2,1)S(1)}, bf16[2,6,1,1,384,256]{5,4,3,2,1,0:T(8,128)(2,1)S(1)}, u32[]{:S(2)}, u32[]{:S(2)}) collective-permute-start(bf16[2,6,1,1,384,256]{5,4,3,2,1,0:T(8,128)(2,1)S(1)} %pad_maximum_fusion.3), channel_id=1, source_target_pairs={{8,0},{16,8},{24,16},{32,24},{40,32},{48,40},{56,48},{9,1},{17,9},... | collective-permute-start | bytes 7077896 | tf_op jit(solution)/shard_map/ppermute | solution.py:21
  99.3 3.9 copy-start.1
  103.2 3.7 copy-start.2
  106.9 154.8 %collective-permute-start.4 = (bf16[2,6,3,1,384,256]{5,4,3,2,1,0:T(8,128)(2,1)}, bf16[2,6,3,1,384,256]{5,4,3,2,1,0:T(8,128)(2,1)}, u32[]{:S(2)}, u32[]{:S(2)}) collective-permute-start(bf16[2,6,3,1,384,256]{5,4,3,2,1,0:T(8,128)(2,1)} %pad_maximum_fusion.1), channel_id=1, source_target_pairs={{0,1},{1,2},{2,3},{3,4},{4,5},{5,6},{6,7},{8,9},{9,10},{10,11},{11... | collective-permute-start | bytes 21233672 | tf_op jit(solution)/shard_map/ppermute | solution.py:20
  114.1 301.5 %collective-permute-start.5 = (bf16[2,6,3,1,384,256]{5,4,3,2,1,0:T(8,128)(2,1)}, bf16[2,6,3,1,384,256]{5,4,3,2,1,0:T(8,128)(2,1)}, u32[]{:S(2)}, u32[]{:S(2)}) collective-permute-start(bf16[2,6,3,1,384,256]{5,4,3,2,1,0:T(8,128)(2,1)} %pad_maximum_fusion.1), channel_id=1, source_target_pairs={{1,0},{2,1},{3,2},{4,3},{5,4},{6,5},{7,6},{9,8},{10,9},{11,10},{12... | collective-permute-start | bytes 21233672 | tf_op jit(solution)/shard_map/ppermute | solution.py:21
where the time goes:
time: 720 us; the launch traced here: 716 us
  waiting for transfers between devices  353 us (49%)
  matrix products  149 us (21%)
  other arithmetic  81.5 us (11%)
  local copies, waits for them, and re-layouts  51.5 us (7%)
  blocking collectives  50.6 us (7%)
  starting transfers between devices  17.4 us (2%)
  loops' own time  13.1 us (2%)
    ppermute x3, waiting for transfers between devices, padded(): before = lax.ppermute(last, axis, up)  194 us
    ppermute x3, waiting for transfers between devices, padded(): after = lax.ppermute(initial, axis, down)  159 us
    dot_general x8, matrix products, head_attention(): jnp.einsum('qd,kd->qk', query_part, key_part, preferred_element_type=jnp....  76.2 us
    dot_general x8, matrix products, head_attention(): summed = jnp.dot(weights, value_part, preferred_element_type=jnp.float32)  72.6 us
    reduce_sum x8, other arithmetic, head_attention(): totals = jnp.sum(expon, axis=1, keepdims=True)  62.1 us
    dynamic_slice x4, local copies, waits for them, and re-layouts, attend_tile(): lax.dynamic_slice_in_dim(extended, tile_idx, 3, 1)  37.6 us
    all_to_all x1, blocking collectives, per_device(): lax.all_to_all(jnp.stack([queries, key_field, value_field]), 'ha', split_...  35.1 us
    concatenate x3, other arithmetic, padded(): shard = jnp.concatenate([before, shard, after], axis=dim)  18.4 us
  transfers between devices with their start and end apart: 6, of which 5 were waited for; matrix products, arithmetic and copies ran while one was open for 0% of the time, Pallas kernels for 0%

commit v1 on v0

v1 whole, which is shorter than its diff:
```python
import functools

import jax
import jax.numpy as jnp
from jax import lax
from jax.experimental import pallas as pl
from jax.experimental.pallas import tpu as pltpu
from jax.sharding import PartitionSpec as P

HEAD = 128
HEADS = 2
ROWS = 8
FR = 3
LINE = 64
TOK = FR * LINE
FACTOR = HEAD**-0.5 * 1.4426950408889634
MESH = pl.DeviceIdType.MESH
BF = jnp.bfloat16
F32 = jnp.float32

A, D, E, B, C, F = range(6)
STREAMS = ("kr", "kl", "vr", "vl", "kf", "vf", "qb", "qc", "qd0", "qd1", "qe", "qf")
RETURNS = {B: 0, C: 1, D: 2, E: 3, F: 4}
LOCAL = {A: 0, D: 1, C: 2}


def rows_of(chunk):
    return pl.ds(pl.multiple_of(chunk * LINE, LINE), LINE)


def inside(chunk):
    return (chunk >= 0) & (chunk < ROWS)


def merge(parts):
    top = functools.reduce(jnp.maximum, [log for _, log in parts])
    shares = [jnp.exp2(log - top) for _, log in parts]
    total = functools.reduce(jnp.add, shares)
    value = functools.reduce(jnp.add, [share * out for share, (out, _) in zip(shares, parts)])
    return value / total, top + jnp.log2(total)


def kernel(
    q_in, k_in, v_in, out, kbuf, vbuf, qbuf, okeep, lkeep, osend, lsend, orecv, lrecv, local_sem, send_sem, recv_sem,
    osend_sem, orecv_sem, lsend_sem, lrecv_sem
):
    core = lax.axis_index("ta")
    ha = lax.axis_index("ha")
    wa = lax.axis_index("wa")
    z, x_lo, y, x_hi = ha % 4, ha // 4, wa // 2, wa % 2
    zt = z // 2

    def device(lo, hi, yy, zz, cc):
        return {"ta": cc, "ha": lo * 4 + zz, "wa": yy * 2 + hi}

    swap = 1 - (x_lo + zt) % 2
    out_core = (core + swap) % 2
    in_core = (core + 1 - swap) % 2
    has_other = (swap == 1) | (core == zt)
    sends_other = (swap == 0) | (core != zt)
    right = device(x_lo, x_hi, y, (z + 1) % 4, core)
    left = device(x_lo, x_hi, y, (z + 3) % 4, core)
    step_y = 1 - 2 * x_hi
    y_next = device(x_lo, x_hi, (y + step_y + 4) % 4, z, core)
    y_prev = device(x_lo, x_hi, (y - step_y + 4) % 4, z, core)
    y_first = 3 * x_hi
    has_prev = y != y_first
    has_next = y != 3 - y_first
    near_out = device(1 - x_lo, x_hi, y, z, out_core)
    near_in = device(1 - x_lo, x_hi, y, z, in_core)
    diag_out = device(1 - x_lo, 1 - x_hi, y, z, out_core)
    diag_in = device(1 - x_lo, 1 - x_hi, y, z, in_core)
    across = device(x_lo, 1 - x_hi, y, z, core)

    barrier = pltpu.get_barrier_semaphore()
    peers = (right, left, y_next, y_prev, near_out, near_in, diag_out, diag_in, across)
    for peer in peers:
        pl.semaphore_signal(barrier, inc=1, device_id=peer, device_id_type=MESH)
    pl.semaphore_wait(barrier, len(peers))

    def remote(stream, chunk, src, dst, target):
        at = STREAMS.index(stream)
        return pltpu.make_async_remote_copy(
            src_ref=src, dst_ref=dst, send_sem=send_sem.at[at, chunk], recv_sem=recv_sem.at[at, chunk],
            device_id=target, device_id_type=MESH
        )

    def part(ref, *lead, chunk, lanes=pl.ds(0, 2 * HEAD)):
        return ref.at[(*lead, slice(None), rows_of(chunk), lanes)]

    first, second = pl.ds(0, HEAD), pl.ds(HEAD, HEAD)

    def copy(stream, chunk):
        if stream in ("kr", "kl"):
            return remote(stream, chunk, part(k_in, chunk=chunk), part(kbuf, z, chunk=chunk), right if stream == "kr" else left)
        if stream in ("vr", "vl"):
            return remote(stream, chunk, part(v_in, chunk=chunk), part(vbuf, z, chunk=chunk), right if stream == "vr" else left)
        if stream == "kf":
            slab = (z + 3) % 4
            return remote(stream, chunk, part(kbuf, slab, chunk=chunk), part(kbuf, slab, chunk=chunk), right)
        if stream == "vf":
            slab = (z + 1) % 4
            return remote(stream, chunk, part(vbuf, slab, chunk=chunk), part(vbuf, slab, chunk=chunk), left)
        if stream == "qb":
            return remote(stream, chunk, part(q_in, chunk=chunk), part(qbuf, B, chunk=chunk), near_out)
        if stream == "qc":
            return remote(stream, chunk, part(q_in, chunk=chunk), part(qbuf, C, chunk=chunk), diag_out)
        if stream == "qd0":
            return remote(stream, chunk, part(qbuf, B, chunk=chunk, lanes=first), part(qbuf, D, chunk=chunk, lanes=first), diag_in)
        if stream == "qd1":
            return remote(stream, chunk, part(qbuf, C, chunk=chunk, lanes=second), part(qbuf, D, chunk=chunk, lanes=second), near_in)
        if stream == "qe":
            return remote(stream, chunk, part(qbuf, D, chunk=chunk), part(qbuf, E, chunk=chunk), y_next)
        return remote(stream, chunk, part(qbuf, C, chunk=chunk), part(qbuf, F, chunk=chunk), y_next)

    def arrival(stream, chunk):
        if stream in ("kr", "kl", "kf"):
            slab = (z + {"kr": 3, "kl": 1, "kf": 2}[stream]) % 4
            ref = part(kbuf, slab, chunk=chunk)
        elif stream in ("vr", "vl", "vf"):
            slab = (z + {"vr": 3, "vl": 1, "vf": 2}[stream]) % 4
            ref = part(vbuf, slab, chunk=chunk)
        elif stream == "qd0":
            ref = part(qbuf, D, chunk=chunk, lanes=first)
        elif stream == "qd1":
            ref = part(qbuf, D, chunk=chunk, lanes=second)
        else:
            ref = part(qbuf, {"qb": B, "qc": C, "qe": E, "qf": F}[stream], chunk=chunk)
        return remote(stream, chunk, ref, ref, right)

    def returns(kind, chunk, target):
        at = RETURNS[kind]
        return (
            pltpu.make_async_remote_copy(
                src_ref=osend.at[at, chunk], dst_ref=orecv.at[at, chunk], send_sem=osend_sem.at[at, chunk],
                recv_sem=orecv_sem.at[at, chunk], device_id=target, device_id_type=MESH
            ),
            pltpu.make_async_remote_copy(
                src_ref=lsend.at[at, chunk], dst_ref=lrecv.at[at, chunk], send_sem=lsend_sem.at[at, chunk],
                recv_sem=lrecv_sem.at[at, chunk], device_id=target, device_id_type=MESH
            ),
        )

    back = {B: near_in, C: diag_in, D: across, E: y_prev, F: y_prev}

    def start_own(chunk):
        for stream in ("kr", "kl", "vr", "vl", "qb", "qc"):
            copy(stream, chunk).start()

    def send_back(kind, chunk, values, logs):
        at = RETURNS[kind]
        for head in range(HEADS):
            osend[at, chunk, :, head * HEAD : (head + 1) * HEAD] = values[head].astype(BF)
        stacked = jnp.concatenate(logs, axis=0)
        for block in range(3):
            lsend[at, chunk, block : block + 1, :] = stacked[block * HEAD : (block + 1) * HEAD].T[0:1, :]
        for one in returns(kind, chunk, back[kind]):
            one.start()

    def came_back(kind, chunk):
        at = RETURNS[kind]
        for one in returns(kind, chunk, back[kind]):
            one.wait_recv()
        blocks = [
            jnp.broadcast_to(lrecv[at, chunk, block : block + 1, :], (HEAD, HEAD)).T for block in range(3)
        ]
        stacked = jnp.concatenate(blocks, axis=0)
        return [
            (orecv[at, chunk, :, head * HEAD : (head + 1) * HEAD].astype(F32), stacked[head * TOK : (head + 1) * TOK])
            for head in range(HEADS)
        ]

    def kept(kind, chunk):
        at = LOCAL[kind]
        return [(okeep[at, chunk, head], lkeep[at, chunk, head]) for head in range(HEADS)]

    def attend(chunk, begin, span, sets, slabs):
        keys = pl.ds(pl.multiple_of(begin, LINE), span * LINE)
        count = FR * span * LINE
        ones = jnp.ones((count, HEAD), BF)
        results = {kind: [] for kind in sets}
        for head in range(HEADS):
            lanes = pl.ds(head * HEAD, HEAD)
            queries = qbuf[sets[0] : sets[0] + 3, :, rows_of(chunk), lanes].reshape(3 * TOK, HEAD)
            scores = [
                lax.dot_general(
                    queries, kbuf[slab, :, keys, lanes].reshape(count, HEAD), (((1,), (1,)), ((), ())),
                    preferred_element_type=F32
                )
                for slab in slabs
            ]
            top = functools.reduce(jnp.maximum, [jnp.max(one, axis=1, keepdims=True) for one in scores]) * FACTOR
            summed = None
            for slab, one in zip(slabs, scores):
                weights = jnp.exp2(one * FACTOR - top).astype(BF)
                values = jnp.concatenate([vbuf[slab, :, keys, lanes].reshape(count, HEAD), ones], axis=1)
                product = jnp.dot(weights, values, preferred_element_type=F32)
                summed = product if summed is None else summed + product
            totals = summed[:, HEAD:]
            mean = summed[:, :HEAD] / totals
            logs = top + jnp.log2(totals)
            for at, kind in enumerate(sets):
                results[kind].append((mean[at * TOK : (at + 1) * TOK], logs[at * TOK : (at + 1) * TOK]))
        for kind in sets:
            if kind in LOCAL:
                for head in range(HEADS):
                    okeep[LOCAL[kind], chunk, head], lkeep[LOCAL[kind], chunk, head] = results[kind][head]
            elif kind == B:
                send_back(kind, chunk, *zip(*results[kind]))
            else:

                @pl.when(has_prev)
                def _():
                    send_back(kind, chunk, *zip(*results[kind]))

    def attend_both(chunk, begin, span):
        attend(chunk, begin, span, (A, D, E), (0, 1, 2, 3))

        @pl.when(has_other)
        def _():
            attend(chunk, begin, span, (B, C, F), (2 - 2 * zt, 3 - 2 * zt))

    own = [
        pltpu.make_async_copy(k_in, kbuf.at[z], local_sem.at[0]),
        pltpu.make_async_copy(v_in, vbuf.at[z], local_sem.at[1]),
        pltpu.make_async_copy(q_in, qbuf.at[A], local_sem.at[2]),
    ]
    for chunk in range(3):
        start_own(chunk)
    for one in own:
        one.start()

    @pl.when(jnp.logical_not(has_prev))
    def _():
        fill = [
            pltpu.make_async_copy(q_in, qbuf.at[E], local_sem.at[3]),
            pltpu.make_async_copy(q_in, qbuf.at[F], local_sem.at[4]),
        ]
        for one in fill:
            one.start()
        for one in fill:
            one.wait()

    for one in own:
        one.wait()

    def wait_keys(chunk):
        for stream in ("kl", "vr", "kf", "vf"):
            arrival(stream, chunk).wait_recv()

    def step(turn, carry):
        now = turn - 2

        @pl.when((now >= 0) & (now + 3 < ROWS))
        def _():
            start_own(now + 3)

        @pl.when(now + 2 < ROWS)
        def _():
            chunk = now + 2
            arrival("kr", chunk).wait_recv()
            copy("kf", chunk).start()
            arrival("vl", chunk).wait_recv()
            copy("vf", chunk).start()
            arrival("qb", chunk).wait_recv()
            copy("qd0", chunk).start()
            arrival("qc", chunk).wait_recv()
            copy("qd1", chunk).start()

        @pl.when(inside(now + 1))
        def _():
            chunk = now + 1
            arrival("qd0", chunk).wait_recv()
            arrival("qd1", chunk).wait_recv()

            @pl.when(has_next)
            def _():
                copy("qe", chunk).start()

                @pl.when(has_other)
                def _():
                    copy("qf", chunk).start()

        @pl.when(inside(now))
        def _():
            @pl.when(now == 0)
            def _():
                wait_keys(0)

            @pl.when(now + 1 < ROWS)
            def _():
                wait_keys(now + 1)

            @pl.when(has_prev)
            def _():
                arrival("qe", now).wait_recv()

                @pl.when(has_other)
                def _():
                    arrival("qf", now).wait_recv()

            rim = (now == 0) | (now == ROWS - 1)

            @pl.when(rim)
            def _():
                attend_both(now, now // (ROWS - 1) * (ROWS - 2) * LINE, 2)

            @pl.when(jnp.logical_not(rim))
            def _():
                attend_both(now, (now - 1) * LINE, 3)

        @pl.when(inside(now - 1))
        def _():
            chunk = now - 1

            def pass_on(kind, extra):
                @pl.when(has_next)
                def _():
                    merged = [merge(pair) for pair in zip(kept(kind, chunk), came_back(extra, chunk))]
                    send_back(kind, chunk, *zip(*merged))

                @pl.when(jnp.logical_not(has_next))
                def _():
                    send_back(kind, chunk, *zip(*kept(kind, chunk)))

            pass_on(D, E)

            @pl.when(has_other)
            def _():
                pass_on(C, F)

        @pl.when(now - 2 >= 0)
        def _():
            chunk = now - 2

            def finish(kinds):
                parts = [kept(A, chunk)] + [came_back(kind, chunk) for kind in kinds]
                for head in range(HEADS):
                    value, _ = merge([one[head] for one in parts])
                    out[:, rows_of(chunk), head * HEAD : (head + 1) * HEAD] = value.astype(BF).reshape(FR, LINE, HEAD)

            @pl.when(sends_other)
            def _():
                finish((D, B, C))

            @pl.when(jnp.logical_not(sends_other))
            def _():
                finish((D,))

        return carry

    lax.fori_loop(0, ROWS + 4, step, 0)

    def drain(chunk, carry):
        for stream in ("kr", "kl", "vr", "vl", "kf", "vf", "qb", "qc", "qd0", "qd1"):
            copy(stream, chunk).wait_send()

        def sent(kind):
            for one in returns(kind, chunk, back[kind]):
                one.wait_send()

        sent(D)

        @pl.when(has_other)
        def _():
            sent(B)
            sent(C)

            @pl.when(has_prev)
            def _():
                sent(F)

            @pl.when(has_next)
            def _():
                copy("qf", chunk).wait_send()

        @pl.when(has_prev)
        def _():
            sent(E)

        @pl.when(has_next)
        def _():
            copy("qe", chunk).wait_send()

        return carry

    lax.fori_loop(0, ROWS, drain, 0)


def per_device(queries, key_field, value_field):
    shape = queries.shape
    flat = (FR, ROWS * LINE, HEADS * HEAD)
    args = [one.reshape(flat) for one in (queries, key_field, value_field)]
    anywhere = pl.BlockSpec(memory_space=pl.ANY)
    result = pl.pallas_call(
        kernel,
        out_shape=jax.ShapeDtypeStruct(flat, BF),
        in_specs=[anywhere] * 3,
        out_specs=pl.BlockSpec(memory_space=pltpu.VMEM),
        scratch_shapes=[
            pltpu.VMEM((4, *flat), BF),
            pltpu.VMEM((4, *flat), BF),
            pltpu.VMEM((6, *flat), BF),
            pltpu.VMEM((3, ROWS, HEADS, TOK, HEAD), F32),
            pltpu.VMEM((3, ROWS, HEADS, TOK, HEAD), F32),
            pltpu.VMEM((5, ROWS, TOK, HEADS * HEAD), BF),
            pltpu.VMEM((5, ROWS, 8, HEAD), F32),
            pltpu.VMEM((5, ROWS, TOK, HEADS * HEAD), BF),
            pltpu.VMEM((5, ROWS, 8, HEAD), F32),
            pltpu.SemaphoreType.DMA((5,)),
            pltpu.SemaphoreType.DMA((len(STREAMS), ROWS)),
            pltpu.SemaphoreType.DMA((len(STREAMS), ROWS)),
            pltpu.SemaphoreType.DMA((5, ROWS)),
            pltpu.SemaphoreType.DMA((5, ROWS)),
            pltpu.SemaphoreType.DMA((5, ROWS)),
            pltpu.SemaphoreType.DMA((5, ROWS)),
        ],
        compiler_params=pltpu.CompilerParams(
            collective_id=0, has_side_effects=True, vmem_limit_bytes=60 * 2**20
        ),
        name="tile_attention",
    )(*args)
    return result.reshape(shape)


def solution(mesh):
    spec = P(("ta", "ha"), None, "wa", None)
    return jax.shard_map(per_device, mesh=mesh, in_specs=(spec,) * 3, out_specs=spec, check_vma=False)
```

time: 720 us -> 103 us (0.14)
  waiting for transfers between devices: 353 us -> 0 us
  matrix products: 149 us -> 0 us
  Pallas kernels: 0 us -> 101 us
  other arithmetic: 81.5 us -> 0 us
  blocking collectives: 50.6 us -> 0 us
  local copies, waits for them, and re-layouts: 51.5 us -> 2.06 us
  starting transfers between devices: 17.4 us -> 0 us
  loops' own time: 13.1 us -> 0 us
    ppermute x6 -> x0, waiting for transfers between devices: 353 us -> none  [the longest x3 194 us: padded(): before = lax.ppermute(last, axis, up)]
    dot_general x16 -> x0, matrix products: 149 us -> none  [the longest x8 76.2 us: head_attention(): jnp.einsum('qd,kd->qk', query_part, key_part, preferred_element_type=jnp....]
    pallas_call x0 -> x1, Pallas kernels: none -> 101 us  [per_device(): pl.pallas_call(kernel, out_shape=jax.ShapeDtypeStruct(flat, BF), in_specs...]
    reduce_sum x8 -> x0, other arithmetic: 62.1 us -> none  [head_attention(): totals = jnp.sum(expon, axis=1, keepdims=True)]
    all_to_all x2 -> x0, blocking collectives: 50.6 us -> none  [the longest x1 35.1 us: per_device(): lax.all_to_all(jnp.stack([queries, key_field, value_field]), 'ha', split_...]
    dynamic_slice x12 -> x0, local copies, waits for them, and re-layouts: 40.5 us -> none  [the longest x4 37.6 us: attend_tile(): lax.dynamic_slice_in_dim(extended, tile_idx, 3, 1)]
    concatenate x3 -> x0, other arithmetic: 18.4 us -> none  [padded(): shard = jnp.concatenate([before, shard, after], axis=dim)]
    ppermute x6 -> x0, starting transfers between devices: 17.4 us -> none  [the longest x3 10.5 us: padded(): before = lax.ppermute(last, axis, up)]
  transfers between devices with their start and end apart: 6 -> 0, of which waited for: 5 -> 0; matrix products, arithmetic and copies ran while one was open for 0% -> 0% of each run, Pallas kernels for 0% -> 0%
where the time goes in v1:
time: 103 us
  Pallas kernels  101 us (98%)
  local copies, waits for them, and re-layouts  2.06 us (2%)
    pallas_call x1, Pallas kernels, per_device(): pl.pallas_call(kernel, out_shape=jax.ShapeDtypeStruct(flat, BF), in_specs...  101 us
    unnamed x1, local copies, waits for them, and re-layouts  2.06 us

profile of v1, /device:TPU:1, one launch (start us, length us, event | category | flops | bytes accessed | tf_op | source)
XLA Modules:
  0.0 102.8 jit_solution(9918051789860067412)
XLA Ops:
  0.0 100.8 %tile_attention.1 = bf16[3,512,256]{2,1,0:T(8,128)(2,1)} custom-call(bf16[3,512,256]{2,1,0:T(8,128)(2,1)} %bitcast.5, bf16[3,512,256]{2,1,0:T(8,128)(2,1)} %bitcast.6, bf16[3,512,256]{2,1,0:T(8,128)(2,1)} %bitcast.7), custom_call_target="tpu_custom_call" | custom-call | tf_op jit(solution)/shard_map/tile_attention/pallas_call | solution.py:395
  100.8 2.1 %copy.5 = bf16[3,64,8,256]{3,2,1,0:T(8,128)(2,1)} copy(bf16[3,64,8,256]{3,2,1,0:T(8,128)(2,1)} %bitcast.4) | data formatting | bytes 1572864

commit v2 on v1

v2 whole, which is shorter than its diff:
```python
import functools

import jax
import jax.numpy as jnp
from jax import lax
from jax.experimental import pallas as pl
from jax.experimental.pallas import tpu as pltpu
from jax.sharding import PartitionSpec as P

HEAD = 128
HEADS = 2
ROWS = 8
FR = 3
LINE = 64
HALF = LINE // 2
TOK = FR * LINE
FACTOR = HEAD**-0.5 * 1.4426950408889634
MESH = pl.DeviceIdType.MESH
BF = jnp.bfloat16
F32 = jnp.float32

A, D, E, B, C, F = range(6)
BLOCK = 768
STREAMS = ("kr", "kl", "vr", "vl", "kf", "vf", "qb", "qc", "qd0", "qd1", "qe", "qf")
RETURNS = {B: 0, C: 1, D: 2, E: 3, F: 4}
LOCAL = {A: 0, D: 1, C: 2}


def rows_of(chunk):
    return pl.ds(pl.multiple_of(chunk * LINE, LINE), LINE)


def merge(parts):
    top = functools.reduce(jnp.maximum, [log for _, log in parts])
    shares = [jnp.exp2(log - top) for _, log in parts]
    total = functools.reduce(jnp.add, shares)
    value = functools.reduce(jnp.add, [share * out for share, (out, _) in zip(shares, parts)])
    return value / total, top + jnp.log2(total)


def kernel(
    q_in, k_in, v_in, out, kbuf, vbuf, qbuf, okeep, lkeep, osend, lsend, orecv, lrecv, local_sem, send_sem, recv_sem,
    osend_sem, orecv_sem, lsend_sem, lrecv_sem, done, out_sem
):
    core = lax.axis_index("ta")
    ha = lax.axis_index("ha")
    wa = lax.axis_index("wa")
    z, x_lo, y, x_hi = ha % 4, ha // 4, wa // 2, wa % 2
    zt = z // 2

    def device(lo, hi, yy, zz, cc):
        return {"ta": cc, "ha": lo * 4 + zz, "wa": yy * 2 + hi}

    swap = 1 - (x_lo + zt) % 2
    out_core = (core + swap) % 2
    in_core = (core + 1 - swap) % 2
    has_other = (swap == 1) | (core == zt)
    sends_other = (swap == 0) | (core != zt)
    right = device(x_lo, x_hi, y, (z + 1) % 4, core)
    left = device(x_lo, x_hi, y, (z + 3) % 4, core)
    step_y = 1 - 2 * x_hi
    y_next = device(x_lo, x_hi, (y + step_y + 4) % 4, z, core)
    y_prev = device(x_lo, x_hi, (y - step_y + 4) % 4, z, core)
    y_first = 3 * x_hi
    has_prev = y != y_first
    has_next = y != 3 - y_first
    near_out = device(1 - x_lo, x_hi, y, z, out_core)
    near_in = device(1 - x_lo, x_hi, y, z, in_core)
    diag_out = device(1 - x_lo, 1 - x_hi, y, z, out_core)
    diag_in = device(1 - x_lo, 1 - x_hi, y, z, in_core)
    across = device(x_lo, 1 - x_hi, y, z, core)

    barrier = pltpu.get_barrier_semaphore()
    peers = (right, left, y_next, y_prev, near_out, near_in, diag_out, diag_in, across)
    for peer in peers:
        pl.semaphore_signal(barrier, inc=1, device_id=peer, device_id_type=MESH)
    pl.semaphore_wait(barrier, len(peers))

    def remote(stream, chunk, src, dst, target):
        at = STREAMS.index(stream)
        return pltpu.make_async_remote_copy(
            src_ref=src, dst_ref=dst, send_sem=send_sem.at[at, chunk], recv_sem=recv_sem.at[at, chunk],
            device_id=target, device_id_type=MESH
        )

    def part(ref, *lead, chunk, half=None):
        rows = rows_of(chunk) if half is None else pl.ds(pl.multiple_of(chunk * LINE + half * HALF, HALF), HALF)
        return ref.at[(*lead, slice(None), rows, slice(None))]

    def copy(stream, chunk):
        if stream in ("kr", "kl"):
            return remote(stream, chunk, part(k_in, chunk=chunk), part(kbuf, z, chunk=chunk), right if stream == "kr" else left)
        if stream in ("vr", "vl"):
            return remote(stream, chunk, part(v_in, chunk=chunk), part(vbuf, z, chunk=chunk), right if stream == "vr" else left)
        if stream == "kf":
            slab = (z + 3) % 4
            return remote(stream, chunk, part(kbuf, slab, chunk=chunk), part(kbuf, slab, chunk=chunk), right)
        if stream == "vf":
            slab = (z + 1) % 4
            return remote(stream, chunk, part(vbuf, slab, chunk=chunk), part(vbuf, slab, chunk=chunk), left)
        if stream == "qb":
            return remote(stream, chunk, part(q_in, chunk=chunk), part(qbuf, B, chunk=chunk), near_out)
        if stream == "qc":
            return remote(stream, chunk, part(q_in, chunk=chunk), part(qbuf, C, chunk=chunk), diag_out)
        if stream == "qd0":
            return remote(stream, chunk, part(qbuf, B, chunk=chunk, half=0), part(qbuf, D, chunk=chunk, half=0), diag_in)
        if stream == "qd1":
            return remote(stream, chunk, part(qbuf, C, chunk=chunk, half=1), part(qbuf, D, chunk=chunk, half=1), near_in)
        if stream == "qe":
            return remote(stream, chunk, part(qbuf, D, chunk=chunk), part(qbuf, E, chunk=chunk), y_next)
        return remote(stream, chunk, part(qbuf, C, chunk=chunk), part(qbuf, F, chunk=chunk), y_next)

    def arrival(stream, chunk):
        if stream in ("kr", "kl", "kf"):
            slab = (z + {"kr": 3, "kl": 1, "kf": 2}[stream]) % 4
            ref = part(kbuf, slab, chunk=chunk)
        elif stream in ("vr", "vl", "vf"):
            slab = (z + {"vr": 3, "vl": 1, "vf": 2}[stream]) % 4
            ref = part(vbuf, slab, chunk=chunk)
        elif stream == "qd0":
            ref = part(qbuf, D, chunk=chunk, half=0)
        elif stream == "qd1":
            ref = part(qbuf, D, chunk=chunk, half=1)
        else:
            ref = part(qbuf, {"qb": B, "qc": C, "qe": E, "qf": F}[stream], chunk=chunk)
        return remote(stream, chunk, ref, ref, right)

    def returns(kind, chunk, target):
        at = RETURNS[kind]
        return (
            pltpu.make_async_remote_copy(
                src_ref=osend.at[at, chunk], dst_ref=orecv.at[at, chunk], send_sem=osend_sem.at[at, chunk],
                recv_sem=orecv_sem.at[at, chunk], device_id=target, device_id_type=MESH
            ),
            pltpu.make_async_remote_copy(
                src_ref=lsend.at[at, chunk], dst_ref=lrecv.at[at, chunk], send_sem=lsend_sem.at[at, chunk],
                recv_sem=lrecv_sem.at[at, chunk], device_id=target, device_id_type=MESH
            ),
        )

    back = {B: near_in, C: diag_in, D: across, E: y_prev, F: y_prev}

    def start_own(chunk):
        for stream in ("kr", "kl", "vr", "vl", "qb", "qc"):
            copy(stream, chunk).start()

    lane = lax.broadcasted_iota(jnp.int32, (HEAD, HEAD), 1)
    eye = lane == lax.broadcasted_iota(jnp.int32, (HEAD, HEAD), 0)

    def put_back(kind, slot, head, value, log):
        at = RETURNS[kind]
        osend[at, slot, :, head * HEAD : (head + 1) * HEAD] = value.astype(BF)
        for half, (begin, size) in enumerate(((0, HEAD), (HEAD, TOK - HEAD))):
            picked = jnp.where(eye[:size], log[begin : begin + size], 0.0)
            row = 2 * head + half
            lsend[at, slot, row : row + 1, :] = jnp.sum(picked, axis=0, keepdims=True)

    def came_back(kind, slot, head):
        at = RETURNS[kind]
        logs = []
        for half, size in enumerate((HEAD, TOK - HEAD)):
            row = 2 * head + half
            spread = jnp.broadcast_to(lrecv[at, slot, row : row + 1, :], (size, HEAD))
            logs.append(jnp.sum(jnp.where(eye[:size], spread, 0.0), axis=1, keepdims=True))
        log = jnp.broadcast_to(jnp.concatenate(logs, axis=0), (TOK, HEAD))
        return orecv[at, slot, :, head * HEAD : (head + 1) * HEAD].astype(F32), log

    def kept(kind, slot, head):
        return okeep[LOCAL[kind], slot, head], lkeep[LOCAL[kind], slot, head]

    def pass_on(slot, head):
        for kind, extra in ((D, E), (C, F)):
            put_back(kind, slot, head, *merge([kept(kind, slot, head), came_back(extra, slot, head)]))

    def finish(slot, head):
        parts = [kept(A, slot, head)] + [came_back(kind, slot, head) for kind in (D, B, C)]
        value, _ = merge(parts)
        done[slot, :, :, head * HEAD : (head + 1) * HEAD] = value.astype(BF).reshape(FR, LINE, HEAD)

    def attend(chunk, begin, span, extras):
        keys = pl.ds(pl.multiple_of(begin, LINE), span * LINE)
        groups = (((A, D, E), (0, 1, 2, 3)), ((B, C, F), (2 - 2 * zt, 3 - 2 * zt)))
        jobs = [(sets, slabs, head) for sets, slabs in groups for head in range(HEADS)]

        def pieces(ref, slabs, lanes):
            whole = jnp.concatenate(
                [ref[slab, :, keys, lanes].reshape(FR * span * LINE, HEAD) for slab in slabs], axis=0
            )
            return [whole[at : at + BLOCK] for at in range(0, whole.shape[0], BLOCK)]

        def products(job):
            sets, slabs, head = job
            lanes = pl.ds(head * HEAD, HEAD)
            queries = qbuf[sets[0] : sets[0] + 3, :, rows_of(chunk), lanes].reshape(3 * TOK, HEAD)
            return [
                lax.dot_general(queries, piece, (((1,), (1,)), ((), ())), preferred_element_type=F32)
                for piece in pieces(kbuf, slabs, lanes)
            ]

        scores = products(jobs[0])
        for number, (sets, slabs, head) in enumerate(jobs):
            later = products(jobs[number + 1]) if number + 1 < len(jobs) else None
            columns = [one[:, at : at + HEAD] for one in scores for at in range(0, one.shape[1], HEAD)]
            top = jnp.max(functools.reduce(jnp.maximum, columns), axis=1, keepdims=True) * FACTOR
            summed = None
            for one, piece in zip(scores, pieces(vbuf, slabs, pl.ds(head * HEAD, HEAD))):
                weights = jnp.exp2(one * FACTOR - top).astype(BF)
                product = jnp.dot(
                    weights, jnp.concatenate([piece, jnp.ones_like(piece)], axis=1), preferred_element_type=F32
                )
                summed = product if summed is None else summed + product
            totals = summed[:, HEAD:]
            mean = summed[:, :HEAD] / totals
            logs = top + jnp.log2(totals)
            for at, kind in enumerate(sets):
                value, log = mean[at * TOK : (at + 1) * TOK], logs[at * TOK : (at + 1) * TOK]
                if kind in LOCAL:
                    okeep[LOCAL[kind], chunk, head], lkeep[LOCAL[kind], chunk, head] = value, log
                else:
                    put_back(kind, chunk, head, value, log)
            scores = later
            for extra in extras[number]:
                extra()

    def start_back(kind, chunk):
        for one in returns(kind, chunk, back[kind]):
            one.start()

    def wait_back(kind, chunk):
        for one in returns(kind, chunk, back[kind]):
            one.wait_recv()

    own = [
        pltpu.make_async_copy(k_in, kbuf.at[z], local_sem.at[0]),
        pltpu.make_async_copy(v_in, vbuf.at[z], local_sem.at[1]),
        pltpu.make_async_copy(q_in, qbuf.at[A], local_sem.at[2]),
    ]
    for chunk in range(2):
        start_own(chunk)
    for one in own:
        one.start()

    @pl.when(jnp.logical_not(has_prev))
    def _():
        fill = pltpu.make_async_copy(q_in, qbuf.at[E], local_sem.at[3])
        fill.start()
        fill.wait()

    @pl.when(jnp.logical_not(has_prev & has_other))
    def _():
        fill = pltpu.make_async_copy(q_in, qbuf.at[F], local_sem.at[4])
        fill.start()
        fill.wait()

    def absent(kind):
        def blank(slot, carry):
            orecv[RETURNS[kind], slot] = jnp.zeros((TOK, HEADS * HEAD), BF)
            lrecv[RETURNS[kind], slot] = jnp.full((8, HEAD), -1e30, F32)
            return carry

        lax.fori_loop(0, ROWS, blank, 0)

    @pl.when(jnp.logical_not(has_next))
    def _():
        absent(E)

    @pl.when(jnp.logical_not(has_next & has_other))
    def _():
        absent(F)

    @pl.when(jnp.logical_not(sends_other))
    def _():
        absent(B)
        absent(C)

    for one in own:
        one.wait()

    def forward(chunk):
        arrival("kr", chunk).wait_recv()
        copy("kf", chunk).start()
        arrival("vl", chunk).wait_recv()
        copy("vf", chunk).start()
        arrival("qb", chunk).wait_recv()
        copy("qd0", chunk).start()
        arrival("qc", chunk).wait_recv()
        copy("qd1", chunk).start()

    def forward_across(chunk):
        arrival("qd0", chunk).wait_recv()
        arrival("qd1", chunk).wait_recv()

        @pl.when(has_next)
        def _():
            copy("qe", chunk).start()

            @pl.when(has_other)
            def _():
                copy("qf", chunk).start()

    def wait_keys(chunk):
        for stream in ("kl", "vr", "kf", "vf"):
            arrival(stream, chunk).wait_recv()

    def wait_queries(chunk):
        @pl.when(has_prev)
        def _():
            arrival("qe", chunk).wait_recv()

            @pl.when(has_other)
            def _():
                arrival("qf", chunk).wait_recv()

    def wait_sides(chunk):
        @pl.when(has_next)
        def _():
            wait_back(E, chunk)

            @pl.when(has_other)
            def _():
                wait_back(F, chunk)

    def wait_home(chunk):
        wait_back(D, chunk)

        @pl.when(sends_other)
        def _():
            wait_back(B, chunk)
            wait_back(C, chunk)

    def start_sides(chunk):
        @pl.when(has_prev)
        def _():
            start_back(E, chunk)

            @pl.when(has_other)
            def _():
                start_back(F, chunk)

        @pl.when(has_other)
        def _():
            start_back(B, chunk)

    def start_home(chunk):
        start_back(D, chunk)

        @pl.when(has_other)
        def _():
            start_back(C, chunk)

    def stored(chunk):
        return pltpu.make_async_copy(done.at[chunk], out.at[:, rows_of(chunk), :], out_sem.at[chunk])

    def spare(chunk):
        there = (chunk + ROWS) // ROWS
        return there * chunk + (1 - there) * ROWS

    def merging(passed, finished):
        work = [
            functools.partial(one, slot, head)
            for one, slot in ((pass_on, passed), (finish, finished))
            for head in range(HEADS)
        ]
        return [[one] for one in work]

    forward(0)
    start_own(2)
    forward(1)
    start_own(3)
    forward_across(0)
    forward(2)
    start_own(4)
    forward_across(1)
    wait_keys(0)
    wait_keys(1)
    wait_queries(0)
    attend(0, 0, 2, [[]] * 4)
    start_sides(0)

    def step(now, carry):
        @pl.when(now + 2 < ROWS)
        def _():
            forward(now + 2)

        @pl.when(now + 4 < ROWS)
        def _():
            start_own(now + 4)

        forward_across(now + 1)
        wait_keys(now + 1)
        wait_queries(now)

        @pl.when(now >= 2)
        def _():
            wait_sides(now - 2)

        @pl.when(now >= 4)
        def _():
            wait_home(now - 4)

        attend(now, (now - 1) * LINE, 3, merging(spare(now - 2), spare(now - 4)))
        start_sides(now)

        @pl.when(now >= 2)
        def _():
            start_home(now - 2)

        @pl.when(now >= 4)
        def _():
            stored(now - 4).start()

        return carry

    lax.fori_loop(1, ROWS - 1, step, 0)

    last = ROWS - 1
    wait_queries(last)
    wait_sides(last - 2)
    wait_home(last - 4)
    attend(last, (last - 1) * LINE, 2, merging(last - 2, last - 4))
    start_sides(last)
    start_home(last - 2)
    stored(last - 4).start()

    def pass_last(chunk):
        wait_sides(chunk)
        for head in range(HEADS):
            pass_on(chunk, head)
        start_home(chunk)

    def finish_last(chunk):
        wait_home(chunk)
        for head in range(HEADS):
            finish(chunk, head)
        stored(chunk).start()

    pass_last(last - 1)
    finish_last(last - 3)
    finish_last(last - 2)
    pass_last(last)
    finish_last(last - 1)
    finish_last(last)

    def drain(chunk, carry):
        for stream in ("kr", "kl", "vr", "vl", "kf", "vf", "qb", "qc", "qd0", "qd1"):
            copy(stream, chunk).wait_send()
        stored(chunk).wait()

        def sent(kind):
            for one in returns(kind, chunk, back[kind]):
                one.wait_send()

        sent(D)

        @pl.when(has_other)
        def _():
            sent(B)
            sent(C)

            @pl.when(has_prev)
            def _():
                sent(F)

            @pl.when(has_next)
            def _():
                copy("qf", chunk).wait_send()

        @pl.when(has_prev)
        def _():
            sent(E)

        @pl.when(has_next)
        def _():
            copy("qe", chunk).wait_send()

        return carry

    lax.fori_loop(0, ROWS, drain, 0)


def per_device(queries, key_field, value_field):
    shape = queries.shape
    flat = (FR, ROWS * LINE, HEADS * HEAD)
    args = [one.reshape(flat) for one in (queries, key_field, value_field)]
    anywhere = pl.BlockSpec(memory_space=pl.ANY)
    result = pl.pallas_call(
        kernel,
        out_shape=jax.ShapeDtypeStruct(flat, BF),
        in_specs=[anywhere] * 3,
        out_specs=anywhere,
        scratch_shapes=[
            pltpu.VMEM((4, *flat), BF),
            pltpu.VMEM((4, *flat), BF),
            pltpu.VMEM((6, *flat), BF),
            pltpu.VMEM((3, ROWS + 1, HEADS, TOK, HEAD), F32),
            pltpu.VMEM((3, ROWS + 1, HEADS, TOK, HEAD), F32),
            pltpu.VMEM((5, ROWS + 1, TOK, HEADS * HEAD), BF),
            pltpu.VMEM((5, ROWS + 1, 8, HEAD), F32),
            pltpu.VMEM((5, ROWS + 1, TOK, HEADS * HEAD), BF),
            pltpu.VMEM((5, ROWS + 1, 8, HEAD), F32),
            pltpu.SemaphoreType.DMA((5,)),
            pltpu.SemaphoreType.DMA((len(STREAMS), ROWS)),
            pltpu.SemaphoreType.DMA((len(STREAMS), ROWS)),
            pltpu.SemaphoreType.DMA((5, ROWS)),
            pltpu.SemaphoreType.DMA((5, ROWS)),
            pltpu.SemaphoreType.DMA((5, ROWS)),
            pltpu.SemaphoreType.DMA((5, ROWS)),
            pltpu.VMEM((ROWS + 1, FR, LINE, HEADS * HEAD), BF),
            pltpu.SemaphoreType.DMA((ROWS,)),
        ],
        compiler_params=pltpu.CompilerParams(
            collective_id=0, has_side_effects=True, vmem_limit_bytes=60 * 2**20
        ),
        name="tile_attention",
    )(*args)
    return result.reshape(shape)


def solution(mesh):
    spec = P(("ta", "ha"), None, "wa", None)
    return jax.shard_map(per_device, mesh=mesh, in_specs=(spec,) * 3, out_specs=spec, check_vma=False)
```

time: 103 us -> 95.3 us (0.925)
  Pallas kernels: 101 us -> 93 us
    pallas_call x1, Pallas kernels: 101 us -> 93 us  [per_device(): pl.pallas_call(kernel, out_shape=jax.ShapeDtypeStruct(flat, BF), in_specs...]
where the time goes in v2:
time: 95.3 us; the launch traced here: 95.1 us
  Pallas kernels  93 us (98%)
  local copies, waits for them, and re-layouts  2.06 us (2%)
    pallas_call x1, Pallas kernels, per_device(): pl.pallas_call(kernel, out_shape=jax.ShapeDtypeStruct(flat, BF), in_specs...  93 us
    unnamed x1, local copies, waits for them, and re-layouts  2.06 us

profile of v2, /device:TPU:1, one launch (start us, length us, event | category | flops | bytes accessed | tf_op | source)
XLA Modules:
  0.0 95.1 jit_solution(15918826223934450233)
XLA Ops:
  0.0 93.0 %tile_attention.1 = bf16[3,512,256]{2,1,0:T(8,128)(2,1)} custom-call(bf16[3,512,256]{2,1,0:T(8,128)(2,1)} %bitcast.5, bf16[3,512,256]{2,1,0:T(8,128)(2,1)} %bitcast.6, bf16[3,512,256]{2,1,0:T(8,128)(2,1)} %bitcast.7), custom_call_target="tpu_custom_call" | custom-call | tf_op jit(solution)/shard_map/tile_attention/pallas_call | solution.py:486
  93.0 2.1 %copy.5 = bf16[3,64,8,256]{3,2,1,0:T(8,128)(2,1)} copy(bf16[3,64,8,256]{3,2,1,0:T(8,128)(2,1)} %bitcast.4) | data formatting | bytes 1572864

commit v3 on v2

--- a/solution.py
+++ b/solution.py
@@ -87,7 +87,7 @@
         rows = rows_of(chunk) if half is None else pl.ds(pl.multiple_of(chunk * LINE + half * HALF, HALF), HALF)
         return ref.at[(*lead, slice(None), rows, slice(None))]
 
-    def copy(stream, chunk):
+    def copy(stream, chunk, half=None):
         if stream in ("kr", "kl"):
             return remote(stream, chunk, part(k_in, chunk=chunk), part(kbuf, z, chunk=chunk), right if stream == "kr" else left)
         if stream in ("vr", "vl"):
@@ -99,9 +99,9 @@
             slab = (z + 1) % 4
             return remote(stream, chunk, part(vbuf, slab, chunk=chunk), part(vbuf, slab, chunk=chunk), left)
         if stream == "qb":
-            return remote(stream, chunk, part(q_in, chunk=chunk), part(qbuf, B, chunk=chunk), near_out)
+            return remote(stream, chunk, part(q_in, chunk=chunk, half=half), part(qbuf, B, chunk=chunk, half=half), near_out)
         if stream == "qc":
-            return remote(stream, chunk, part(q_in, chunk=chunk), part(qbuf, C, chunk=chunk), diag_out)
+            return remote(stream, chunk, part(q_in, chunk=chunk, half=half), part(qbuf, C, chunk=chunk, half=half), diag_out)
         if stream == "qd0":
             return remote(stream, chunk, part(qbuf, B, chunk=chunk, half=0), part(qbuf, D, chunk=chunk, half=0), diag_in)
         if stream == "qd1":
@@ -110,7 +110,7 @@
             return remote(stream, chunk, part(qbuf, D, chunk=chunk), part(qbuf, E, chunk=chunk), y_next)
         return remote(stream, chunk, part(qbuf, C, chunk=chunk), part(qbuf, F, chunk=chunk), y_next)
 
-    def arrival(stream, chunk):
+    def arrival(stream, chunk, half=None):
         if stream in ("kr", "kl", "kf"):
             slab = (z + {"kr": 3, "kl": 1, "kf": 2}[stream]) % 4
             ref = part(kbuf, slab, chunk=chunk)
@@ -122,7 +122,7 @@
         elif stream == "qd1":
             ref = part(qbuf, D, chunk=chunk, half=1)
         else:
-            ref = part(qbuf, {"qb": B, "qc": C, "qe": E, "qf": F}[stream], chunk=chunk)
+            ref = part(qbuf, {"qb": B, "qc": C, "qe": E, "qf": F}[stream], chunk=chunk, half=half)
         return remote(stream, chunk, ref, ref, right)
 
     def returns(kind, chunk, target):
@@ -140,9 +140,18 @@
 
     back = {B: near_in, C: diag_in, D: across, E: y_prev, F: y_prev}
 
-    def start_own(chunk):
-        for stream in ("kr", "kl", "vr", "vl", "qb", "qc"):
-            copy(stream, chunk).start()
+    only = {B: 0, C: 1}
+
+    def each_half(whole, *actions):
+        @pl.when(whole)
+        def _():
+            for action in actions:
+                action({B: None, C: None})
+
+        @pl.when(jnp.logical_not(whole))
+        def _():
+            for action in actions:
+                action(only)
 
     lane = lax.broadcasted_iota(jnp.int32, (HEAD, HEAD), 1)
     eye = lane == lax.broadcasted_iota(jnp.int32, (HEAD, HEAD), 0)
@@ -235,55 +244,77 @@
         pltpu.make_async_copy(v_in, vbuf.at[z], local_sem.at[1]),
         pltpu.make_async_copy(q_in, qbuf.at[A], local_sem.at[2]),
     ]
-    for chunk in range(2):
-        start_own(chunk)
-    for one in own:
-        one.start()
-
-    @pl.when(jnp.logical_not(has_prev))
-    def _():
-        fill = pltpu.make_async_copy(q_in, qbuf.at[E], local_sem.at[3])
-        fill.start()
-        fill.wait()
-
-    @pl.when(jnp.logical_not(has_prev & has_other))
-    def _():
-        fill = pltpu.make_async_copy(q_in, qbuf.at[F], local_sem.at[4])
-        fill.start()
-        fill.wait()
-
-    def absent(kind):
-        def blank(slot, carry):
-            orecv[RETURNS[kind], slot] = jnp.zeros((TOK, HEADS * HEAD), BF)
-            lrecv[RETURNS[kind], slot] = jnp.full((8, HEAD), -1e30, F32)
-            return carry
-
-        lax.fori_loop(0, ROWS, blank, 0)
-
-    @pl.when(jnp.logical_not(has_next))
-    def _():
-        absent(E)
-
-    @pl.when(jnp.logical_not(has_next & has_other))
-    def _():
-        absent(F)
-
-    @pl.when(jnp.logical_not(sends_other))
-    def _():
-        absent(B)
-        absent(C)
-
-    for one in own:
-        one.wait()
-
-    def forward(chunk):
+    def start_local():
+        for one in own:
+            one.start()
+        fill_absent()
+
+    def wait_local():
+        for one in own:
+            one.wait()
+
+    def fill_absent():
+        @pl.when(jnp.logical_not(has_prev))
+        def _():
+            fill = pltpu.make_async_copy(q_in, qbuf.at[E], local_sem.at[3])
+            fill.start()
+            fill.wait()
+
+        @pl.when(jnp.logical_not(has_prev & has_other))
+        def _():
+            fill = pltpu.make_async_copy(q_in, qbuf.at[F], local_sem.at[4])
+            fill.start()
+            fill.wait()
+
+        def absent(kind):
+            def blank(slot, carry):
+                orecv[RETURNS[kind], slot] = jnp.zeros((TOK, HEADS * HEAD), BF)
+                lrecv[RETURNS[kind], slot] = jnp.full((8, HEAD), -1e30, F32)
+                return carry
+
+            lax.fori_loop(0, ROWS, blank, 0)
+
+        @pl.when(jnp.logical_not(has_next))
+        def _():
+            absent(E)
+
+        @pl.when(jnp.logical_not(has_next & has_other))
+        def _():
+            absent(F)
+
+        @pl.when(jnp.logical_not(sends_other))
+        def _():
+            absent(B)
+            absent(C)
+
+    def start_kept(chunk):
+        copy("kl", chunk).start()
+        copy("vr", chunk).start()
+
+    def start_passed(chunk):
+        copy("kr", chunk).start()
+        copy("vl", chunk).start()
+
+    def pass_keys(chunk):
         arrival("kr", chunk).wait_recv()
         copy("kf", chunk).start()
         arrival("vl", chunk).wait_recv()
         copy("vf", chunk).start()
-        arrival("qb", chunk).wait_recv()
+
+    def start_queries(chunk):
+        each_half(
+            sends_other,
+            lambda half: copy("qb", chunk, half[B]).start(),
+            lambda half: copy("qc", chunk, half[C]).start(),
+        )
+
+    def pass_queries(chunk):
+        each_half(
+            has_other,
+            lambda half: arrival("qb", chunk, half[B]).wait_recv(),
+            lambda half: arrival("qc", chunk, half[C]).wait_recv(),
+        )
         copy("qd0", chunk).start()
-        arrival("qc", chunk).wait_recv()
         copy("qd1", chunk).start()
 
     def forward_across(chunk):
@@ -363,14 +394,31 @@
         ]
         return [[one] for one in work]
 
-    forward(0)
-    start_own(2)
-    forward(1)
-    start_own(3)
-    forward_across(0)
-    forward(2)
-    start_own(4)
-    forward_across(1)
+    ahead = (
+        (pass_keys, 2),
+        (start_kept, 3),
+        (start_passed, 4),
+        (pass_queries, 2),
+        (start_queries, 4),
+        (forward_across, 1),
+    )
+
+    def serve(now):
+        for action, early in ahead:
+            if isinstance(now, int):
+                if 0 <= now + early < ROWS:
+                    action(now + early)
+            else:
+
+                @pl.when(now + early < ROWS)
+                def _():
+                    action(now + early)
+
+    for turn in range(-max(early for _, early in ahead), 1):
+        serve(turn)
+        if turn == -3:
+            start_local()
+    wait_local()
     wait_keys(0)
     wait_keys(1)
     wait_queries(0)
@@ -378,15 +426,7 @@
     start_sides(0)
 
     def step(now, carry):
-        @pl.when(now + 2 < ROWS)
-        def _():
-            forward(now + 2)
-
-        @pl.when(now + 4 < ROWS)
-        def _():
-            start_own(now + 4)
-
-        forward_across(now + 1)
+        serve(now)
         wait_keys(now + 1)
         wait_queries(now)
 
@@ -442,8 +482,13 @@
     finish_last(last)
 
     def drain(chunk, carry):
-        for stream in ("kr", "kl", "vr", "vl", "kf", "vf", "qb", "qc", "qd0", "qd1"):
+        for stream in ("kr", "kl", "vr", "vl", "kf", "vf", "qd0", "qd1"):
             copy(stream, chunk).wait_send()
+        each_half(
+            sends_other,
+            lambda half: copy("qb", chunk, half[B]).wait_send(),
+            lambda half: copy("qc", chunk, half[C]).wait_send(),
+        )
         stored(chunk).wait()
 
         def sent(kind):

time: 95.3 us -> 93.2 us (0.978)
  Pallas kernels: 93 us -> 90.9 us
    pallas_call x1, Pallas kernels: 93 us -> 90.9 us  [per_device(): pl.pallas_call(kernel, out_shape=jax.ShapeDtypeStruct(flat, BF), in_specs...]
where the time goes in v3:
time: 93.2 us; the launch traced here: 93 us
  Pallas kernels  90.9 us (98%)
  local copies, waits for them, and re-layouts  2.06 us (2%)
    pallas_call x1, Pallas kernels, per_device(): pl.pallas_call(kernel, out_shape=jax.ShapeDtypeStruct(flat, BF), in_specs...  90.9 us
    unnamed x1, local copies, waits for them, and re-layouts  2.06 us

profile of v3, /device:TPU:1, one launch (start us, length us, event | category | flops | bytes accessed | tf_op | source)
XLA Modules:
  0.0 93.0 jit_solution(2895062113430190723)
XLA Ops:
  0.0 90.9 %tile_attention.1 = bf16[3,512,256]{2,1,0:T(8,128)(2,1)} custom-call(bf16[3,512,256]{2,1,0:T(8,128)(2,1)} %bitcast.5, bf16[3,512,256]{2,1,0:T(8,128)(2,1)} %bitcast.6, bf16[3,512,256]{2,1,0:T(8,128)(2,1)} %bitcast.7), custom_call_target="tpu_custom_call" | custom-call | tf_op jit(solution)/shard_map/tile_attention/pallas_call | solution.py:531
  90.9 2.1 %copy.5 = bf16[3,64,8,256]{3,2,1,0:T(8,128)(2,1)} copy(bf16[3,64,8,256]{3,2,1,0:T(8,128)(2,1)} %bitcast.4) | data formatting | bytes 1572864

commit v4 on v3

--- a/solution.py
+++ b/solution.py
@@ -395,11 +395,11 @@
         return [[one] for one in work]
 
     ahead = (
+        (start_queries, 4),
         (pass_keys, 2),
         (start_kept, 3),
         (start_passed, 4),
         (pass_queries, 2),
-        (start_queries, 4),
         (forward_across, 1),
     )
 

time: 93.2 us -> 95.6 us (1.026)
  Pallas kernels: 90.9 us -> 93.3 us
    pallas_call x1, Pallas kernels: 90.9 us -> 93.3 us  [per_device(): pl.pallas_call(kernel, out_shape=jax.ShapeDtypeStruct(flat, BF), in_specs...]
where the time goes in v4:
time: 95.6 us; the launch traced here: 95.4 us
  Pallas kernels  93.3 us (98%)
  local copies, waits for them, and re-layouts  2.06 us (2%)
    pallas_call x1, Pallas kernels, per_device(): pl.pallas_call(kernel, out_shape=jax.ShapeDtypeStruct(flat, BF), in_specs...  93.3 us
    unnamed x1, local copies, waits for them, and re-layouts  2.06 us

profile of v4, /device:TPU:1, one launch (start us, length us, event | category | flops | bytes accessed | tf_op | source)
XLA Modules:
  0.0 95.4 jit_solution(11373630911952517485)
XLA Ops:
  0.0 93.3 %tile_attention.1 = bf16[3,512,256]{2,1,0:T(8,128)(2,1)} custom-call(bf16[3,512,256]{2,1,0:T(8,128)(2,1)} %bitcast.5, bf16[3,512,256]{2,1,0:T(8,128)(2,1)} %bitcast.6, bf16[3,512,256]{2,1,0:T(8,128)(2,1)} %bitcast.7), custom_call_target="tpu_custom_call" | custom-call | tf_op jit(solution)/shard_map/tile_attention/pallas_call | solution.py:531
  93.3 2.1 %copy.5 = bf16[3,64,8,256]{3,2,1,0:T(8,128)(2,1)} copy(bf16[3,64,8,256]{3,2,1,0:T(8,128)(2,1)} %bitcast.4) | data formatting | bytes 1572864
